TPU v7x, 128 devices: a whole 4x4x4 slice. The times are simulated.
128 devices in a mesh: dp: 2 (over z_lo), row: 8 (over x, z_hi), col: 8 (over y, core).
Axes of the slice: x: 4, y: 4, z: 4 (z_hi: 2, z_lo: 2; z = z_hi * 2 + z_lo), core: 2. Of those that a mesh axis runs over, the one named last changes fastest.
Arguments:
- tokens: bfloat16 [384, 8192], P('dp', 'row'), may hold values from -6 to 6
- token_tangent: bfloat16 [384, 8192], P('dp', 'row'), may hold values from -6 to 6
- gate_weight: bfloat16 [8192, 14336], P('row', ('dp', 'col')), may hold values from -0.0625 to 0.0625
- up_weight: bfloat16 [8192, 14336], P('row', ('dp', 'col')), may hold values from -0.0625 to 0.0625
- gate_delta: bfloat16 [8192, 14336], P('row', ('dp', 'col')), may hold values from -0.0625 to 0.0625
- up_delta: bfloat16 [8192, 14336], P('row', ('dp', 'col')), may hold values from -0.0625 to 0.0625
- down_weight: bfloat16 [14336, 8192], P(('dp', 'col'), 'row'), may hold values from -0.046875 to 0.046875
- down_delta: bfloat16 [14336, 8192], P(('dp', 'col'), 'row'), may hold values from -0.046875 to 0.046875
- cotangent: bfloat16 [384, 8192], P(('dp', 'col'), 'row'), may hold values from -6 to 6
Outputs:
- output_primal: bfloat16 [384, 8192], P(('dp', 'col'), 'row')
- output_tangent: bfloat16 [384, 8192], P(('dp', 'col'), 'row')
- input_cotangent: bfloat16 [384, 8192], P(('dp', 'col'), 'row')
- gate_gradient: bfloat16 [8192, 14336], P('row', ('dp', 'col'))
- up_gradient: bfloat16 [8192, 14336], P('row', ('dp', 'col'))
- down_gradient: bfloat16 [14336, 8192], P(('dp', 'col'), 'row')
All inputs are finite; a program needn't handle non-finite values.
Results may differ from a plain program's by a relative error of at most 0.005.
Values may be sent and summed in bfloat16 or wider, within the bound.
A program may use at most 128 MiB of HBM per device.

v0:
```python
import math

import jax
import jax.numpy as jnp
from jax import lax
from jax.sharding import PartitionSpec as P


def silu_pair(gate_sum):
    logistic = jax.nn.sigmoid(gate_sum)
    return (gate_sum * logistic, logistic * (1.0 + gate_sum * (1.0 - logistic)))


def matmul(left_side, right_side):
    return jnp.dot(left_side, right_side, preferred_element_type=jnp.float32)


def matmul_rows(left_side, right_side):
    return lax.dot_general(
        left_side, right_side, (((0,), (0,)), ((), ())), preferred_element_type=jnp.float32
    )


def matmul_trans(left_side, right_side):
    return lax.dot_general(
        left_side, right_side, (((1,), (1,)), ((), ())), preferred_element_type=jnp.float32
    )


def hidden_values(totals):
    gate_sum, up_sum, gate_tangent, up_tangent = totals
    activation, derivative = silu_pair(gate_sum)
    hidden = (activation * up_sum).astype(jnp.bfloat16)
    hidden_tangent = (derivative * gate_tangent * up_sum + activation * up_tangent).astype(
        jnp.bfloat16
    )
    return (hidden, hidden_tangent, (up_sum * derivative, activation))


def forward_block(rows_in, rows_tangent, gate_weight, up_weight, gate_delta, up_delta):
    partials = (
        matmul(rows_in, gate_weight),
        matmul(rows_in, up_weight),
        matmul(rows_in, gate_delta) + matmul(rows_tangent, gate_weight),
        matmul(rows_in, up_delta) + matmul(rows_tangent, up_weight),
    )
    totals = lax.psum((partials[0], partials[1], partials[2], partials[3]), "row")
    hidden, hidden_tangent, saved_units = hidden_values(totals)
    return (hidden, hidden_tangent, saved_units)


def backward_block(cotangent_rows, down_weight, saved_units):
    partial_value = matmul_trans(cotangent_rows, down_weight)
    gate_factor, activation = saved_units
    back_sum = lax.psum(partial_value, "row")
    grad_gate = (back_sum * gate_factor).astype(jnp.bfloat16)
    grad_up = (back_sum * activation).astype(jnp.bfloat16)
    return (grad_gate, grad_up)


def on_device(
    tokens,
    token_tangent,
    gate_weight,
    up_weight,
    gate_delta,
    up_delta,
    down_weight,
    down_delta,
    cotangent,
):
    rows_in, rows_tangent = (
        lax.all_gather(tokens, "dp", axis=0, tiled=True),
        lax.all_gather(token_tangent, "dp", axis=0, tiled=True),
    )
    total_rows = rows_in.shape[0]
    hidden, hidden_tangent, saved_units = forward_block(
        rows_in, rows_tangent, gate_weight, up_weight, gate_delta, up_delta
    )
    feature_count = down_weight.shape[1]
    primal = matmul(hidden, down_weight)
    tangent = matmul(hidden_tangent, down_weight) + matmul(hidden, down_delta)
    summed = lax.psum_scatter(
        jnp.concatenate((primal, tangent), axis=1), ("dp", "col"), scatter_dimension=0, tiled=True
    )
    cotangent_rows = lax.all_gather(cotangent, ("dp", "col"), axis=0, tiled=True)
    output_primal = summed[:, :feature_count].astype(jnp.bfloat16)
    output_tangent = summed[:, feature_count:].astype(jnp.bfloat16)
    grad_gate, grad_up = backward_block(cotangent_rows, down_weight, saved_units)
    normalizer = 1.0 / math.sqrt(total_rows)
    down_partial = matmul_rows(hidden, cotangent_rows)
    gate_partial = matmul_rows(rows_in, grad_gate)
    up_partial = matmul_rows(rows_in, grad_up)
    input_summed = lax.psum_scatter(
        matmul_trans(grad_gate, gate_weight) + matmul_trans(grad_up, up_weight),
        ("dp", "col"),
        scatter_dimension=0,
        tiled=True,
    )
    return (
        output_primal,
        output_tangent,
        input_summed.astype(jnp.bfloat16),
        (gate_partial * normalizer).astype(jnp.bfloat16),
        (up_partial * normalizer).astype(jnp.bfloat16),
        (down_partial * normalizer).astype(jnp.bfloat16),
    )


def solution(mesh):
    placed = (
        P("dp", "row"),
        P("dp", "row"),
        P("row", ("dp", "col")),
        P("row", ("dp", "col")),
        P("row", ("dp", "col")),
        P("row", ("dp", "col")),
        P(("dp", "col"), "row"),
        P(("dp", "col"), "row"),
        P(("dp", "col"), "row"),
    )
    return jax.shard_map(
        on_device,
        mesh=mesh,
        in_specs=placed,
        out_specs=(
            P(("dp", "col"), "row"),
            P(("dp", "col"), "row"),
            P(("dp", "col"), "row"),
            P("row", ("dp", "col")),
            P("row", ("dp", "col")),
            P(("dp", "col"), "row"),
        ),
        check_vma=False,
    )
```

profile of v0, /device:TPU:1, one launch (start us, length us, event | category | flops | bytes accessed | tf_op | source)
XLA Modules:
  0.0 499.9 jit_solution(10085459383905360351)
XLA Ops:
  7.2 12.3 %all_gather.9 = bf16[384,1024]{1,0:T(8,128)(2,1)S(1)} all-gather(bf16[192,1024]{1,0:T(8,128)(2,1)} %param.9), channel_id=1, replica_groups=mesh['dp'=2,'row'=8,'col'=8] {'dp'}, dimensions={0}, use_global_device_ids=true | all-gather | bytes 1179648 | tf_op jit(solution)/shard_map/all_gather | solution.py:73
  19.6 10.2 %all_gather.10 = bf16[384,1024]{1,0:T(8,128)(2,1)S(1)} all-gather(bf16[192,1024]{1,0:T(8,128)(2,1)} %param.10), channel_id=1, replica_groups=mesh['dp'=2,'row'=8,'col'=8] {'dp'}, dimensions={0}, use_global_device_ids=true | all-gather | bytes 1179648 | tf_op jit(solution)/shard_map/all_gather | solution.py:74
  29.8 23.9 %all_gather.11 = bf16[384,1024]{1,0:T(8,128)(2,1)S(1)} all-gather(bf16[24,1024]{1,0:T(8,128)(2,1)S(1)} %copy-done.10), channel_id=1, replica_groups=mesh['dp'=2,'row'=8,'col'=8] {'dp','col'}, dimensions={0}, use_global_device_ids=true | all-gather | bytes 835584 | tf_op jit(solution)/shard_map/all_gather | solution.py:86
  56.8 2.1 fusion.7
  58.8 2.2 fusion.6
  61.0 2.1 convolution_add_fusion.2
  63.0 2.1 convolution_add_fusion.3
  65.1 2.1 fusion.11
  67.2 287.6 %all-reduce.3.cloned.1.call-done = (f32[384,896]{1,0:T(8,128)}, f32[384,896]{1,0:T(8,128)}, f32[384,896]{1,0:T(8,128)}, f32[384,896]{1,0:T(8,128)}, f32[384,896]{1,0:T(8,128)}) async-done(((f32[384,896]{1,0:T(8,128)}, f32[384,896]{1,0:T(8,128)}, f32[384,896]{1,0:T(8,128)}, f32[384,896]{1,0:T(8,128)}, f32[384,896]{1,0:T(8,128)}), (f32[384,896]{1,0:T(8,128)}, f32[384,896]{1,0:T(8,128)}, f32[384,896]{1,0:T(8,128)}, ...) | async-done | bytes 6881296 | tf_op jit(solution)/shard_map/psum | solution.py:47
  354.8 3.9 multiply_convert_fusion.3
  358.7 1.0 fusion.12
  360.5 2.2 convolution_add_fusion
  363.0 2.2 fusion.8
  365.3 2.8 fusion.3
  368.2 1.0 convolution_add_fusion.1
  369.2 2.0 pad_maximum_fusion
  371.3 3.5 fusion.1
  374.8 3.9 copy.16
  378.7 3.5 fusion
  382.2 3.9 copy.15
  386.1 2.4 multiply_convert_fusion
  388.4 37.3 %reduce-scatter.5.cloned.1.call-done = f32[24,1024]{1,0:T(8,128)} async-done(((f32[384,1024]{1,0:T(8,128)}), f32[24,1024]{1,0:T(8,128)}) %reduce-scatter.5.cloned.1.call-update) | async-done | bytes 98320 | tf_op jit(solution)/shard_map/reduce_scatter | solution.py:94
  425.7 1.5 convert_element_type.36
  427.3 64.6 %reduce-scatter.3.cloned.1.call-done = f32[24,2048]{1,0:T(8,128)} async-done(((f32[384,2048]{1,0:T(8,128)}), f32[24,2048]{1,0:T(8,128)}) %reduce-scatter.3.cloned.1.call-update) | async-done | bytes 196624 | tf_op jit(solution)/shard_map/reduce_scatter | solution.py:83
  (44 shorter events, 5.8 us)
Async XLA Ops:
  7.2 57.9 %copy-start = (bf16[896,1024]{1,0:T(8,128)(2,1)S(1)}, bf16[896,1024]{1,0:T(8,128)(2,1)}, u32[]{:S(2)}) copy-start(bf16[896,1024]{1,0:T(8,128)(2,1)} %param.15) | copy-start | bytes 5505028
  7.2 22.6 %copy-start.10 = (bf16[24,1024]{1,0:T(8,128)(2,1)S(1)}, bf16[24,1024]{1,0:T(8,128)(2,1)}, u32[]{:S(2)}) copy-start(bf16[24,1024]{1,0:T(8,128)(2,1)} %param.17) | copy-start | bytes 147460
  7.2 347.6 %all-reduce.3.cloned.1.call-start = ((), (), s32[]{:S(2)}) async-start(), calls=%async_computation.4 | async-start | bytes 13762560 | tf_op jit(solution)/shard_map/psum | solution.py:47
  7.2 46.5 %copy-start.11 = (bf16[1024,896]{1,0:T(8,128)(2,1)S(1)}, bf16[1024,896]{1,0:T(8,128)(2,1)}, u32[]{:S(2)}) copy-start(bf16[1024,896]{1,0:T(8,128)(2,1)} %param.14) | copy-start | bytes 5505028
  19.6 39.3 %copy-start.5 = (bf16[384,1024]{1,0:T(8,128)(2,1)}, bf16[384,1024]{1,0:T(8,128)(2,1)S(1)}, u32[]{:S(2)}) copy-start(bf16[384,1024]{1,0:T(8,128)(2,1)S(1)} %all_gather.9) | copy-start | bytes 2359300
  53.8 1.5 copy-start.12
  55.3 1.5 copy-start.1
  56.8 2.1 copy-start.13
  67.2 358.5 %reduce-scatter.5.cloned.1.call-start = ((), (), s32[]{:S(2)}) async-start(), calls=%async_computation.3 | async-start | bytes 1671168 | tf_op jit(solution)/shard_map/reduce_scatter | solution.py:94
  354.8 3.9 copy-start.14
  358.7 1.0 copy-start.8
  358.7 1.7 copy-start.2
  362.7 129.1 %reduce-scatter.3.cloned.1.call-start = ((), (), s32[]{:S(2)}) async-start(), calls=%async_computation.2 | async-start | bytes 3342336 | tf_op jit(solution)/shard_map/reduce_scatter | solution.py:83
  363.0 2.3 copy-start.3
  363.0 2.3 copy-start.4
  363.0 2.4 copy-start.16
  365.3 2.9 copy-start.6
  365.3 2.9 copy-start.15
  374.8 3.9 copy-start.9
  382.2 3.9 copy-start.7
Sparse Core Ops, SparseCore 0:
  67.3 287.4 all-reduce.2
  362.9 62.8 reduce-scatter.4
  428.3 63.4 reduce-scatter.2
where the time goes:
time: 504 us; the launch traced here: 500 us
  waiting for transfers between devices  389 us (77%)
  blocking collectives  46.5 us (9%)
  matrix products  31 us (6%)
  between operations  13.9 us (3%)
  local copies, waits for them, and re-layouts  10.3 us (2%)
  other arithmetic  8.37 us (2%)
    psum x1, waiting for transfers between devices, forward_block(): lax.psum((partials[0], partials[1], partials[2], partials[3]), 'row')  288 us
    reduce_scatter x1, waiting for transfers between devices, on_device(): lax.psum_scatter(jnp.concatenate((primal, tangent), axis=1), ('dp', 'col'...  64.6 us
    reduce_scatter x1, waiting for transfers between devices, on_device(): lax.psum_scatter(matmul_trans(grad_gate, gate_weight) + matmul_trans(grad...  37.3 us
    all_gather x1, blocking collectives, on_device(): lax.all_gather(cotangent, ('dp', 'col'), axis=0, tiled=True)  23.9 us
    dot_general x9, matrix products, matmul(): return jnp.dot(left_side, right_side, preferred_element_type=jnp.float32)  16.3 us
    all_gather x1, blocking collectives, on_device(): lax.all_gather(tokens, 'dp', axis=0, tiled=True)  12.3 us
    all_gather x1, blocking collectives, on_device(): lax.all_gather(token_tangent, 'dp', axis=0, tiled=True)  10.2 us
  transfers between devices with their start and end apart: 3, of which 3 were waited for; matrix products, arithmetic and copies ran while one was open for 5% of the time, Pallas kernels for 0%

commit v1 on v0

v1 whole, which is shorter than its diff:
```python
import functools
import math

import jax
import jax.numpy as jnp
from jax import lax
from jax.experimental import pallas as pl
from jax.experimental.pallas import tpu as pltpu
from jax.sharding import PartitionSpec as P

BF16 = jnp.bfloat16
F32 = jnp.float32
MESH = pl.DeviceIdType.MESH
TRANS_RIGHT = (((1,), (1,)), ((), ()))
TRANS_LEFT = (((0,), (0,)), ((), ()))


def dot(left_side, right_side):
    return jnp.dot(left_side, right_side, preferred_element_type=F32)


def dot_trans(left_side, right_side):
    return lax.dot_general(left_side, right_side, TRANS_RIGHT, preferred_element_type=F32)


class Copies:
    def __init__(self, send_sems, recv_sems, local_sems):
        self.send_sems, self.recv_sems, self.local_sems = send_sems, recv_sems, local_sems
        self.remote_count = 0
        self.local_count = 0
        self.sent = []

    def start(self, src, dst, device):
        k = self.remote_count
        self.remote_count += 1
        copy = pltpu.make_async_remote_copy(
            src_ref=src,
            dst_ref=dst,
            send_sem=self.send_sems.at[k],
            recv_sem=self.recv_sems.at[k],
            device_id=device,
            device_id_type=MESH,
        )
        copy.start()
        self.sent.append(copy)
        return copy

    def local(self, src, dst):
        k = self.local_count
        self.local_count += 1
        copy = pltpu.make_async_copy(src, dst, self.local_sems.at[k])
        copy.start()
        return copy


class RingSum:
    def __init__(self, copies, me, left, right, block, exact, sent, first, merged, from_left, from_right):
        self.copies, self.left, self.right = copies, left, right
        self.rows = lambda shift: pl.ds(pl.multiple_of(lax.rem(me + shift, 4) * block, 16), block)
        self.exact, self.packed, self.first, self.merged = exact, sent, first, merged
        self.from_left, self.from_right = from_left, from_right

    def start(self):
        far, after, before = self.rows(2), self.rows(1), self.rows(3)
        send = self.copies.start
        self.a0 = send(self.packed.at[0, far], self.first.at[0], self.right)
        self.a1 = send(self.packed.at[1, far], self.first.at[1], self.left)
        self.b1 = send(self.packed.at[1, after], self.from_left.at[1], self.right)
        self.b0 = send(self.packed.at[0, before], self.from_right.at[0], self.left)

    def merge(self):
        send = self.copies.start
        self.a0.wait_recv()
        self.merged[0] = (self.exact[0, self.rows(1)] + self.first[0].astype(F32)).astype(BF16)
        self.c0 = send(self.merged.at[0], self.from_left.at[0], self.right)
        self.a1.wait_recv()
        self.merged[1] = (self.exact[1, self.rows(3)] + self.first[1].astype(F32)).astype(BF16)
        self.c1 = send(self.merged.at[1], self.from_right.at[1], self.left)

    def wait(self):
        for copy in (self.b0, self.b1, self.c0, self.c1):
            copy.wait_recv()

    def total(self, plane):
        return (
            self.exact[plane, self.rows(0)]
            + self.from_left[plane].astype(F32)
            + self.from_right[plane].astype(F32)
        )


class RingGather:
    def __init__(self, copies, me, left, right, block, whole):
        self.copies, self.left, self.right, self.whole = copies, left, right, whole
        self.rows = lambda shift: pl.ds(pl.multiple_of(lax.rem(me + shift, 4) * block, 16), block)

    def send(self, plane, shift, device):
        part = self.whole.at[plane, self.rows(shift)]
        return self.copies.start(part, part, device)

    def start(self):
        self.a0 = self.send(0, 0, self.right)
        self.a1 = self.send(1, 0, self.left)
        self.b1 = self.send(1, 0, self.right)
        self.b0 = self.send(0, 0, self.left)

    def forward(self):
        self.a0.wait_recv()
        self.c0 = self.send(0, 3, self.right)
        self.a1.wait_recv()
        self.c1 = self.send(1, 1, self.left)

    def wait(self):
        for copy in (self.b0, self.b1, self.c0, self.c1):
            copy.wait_recv()


def main_kernel(
    tokens,
    token_tangent,
    gate_weight,
    up_weight,
    gate_delta,
    up_delta,
    down_weight,
    down_delta,
    cotangent,
    primal_out,
    tangent_out,
    input_out,
    hidden_out,
    grad_gate_out,
    grad_up_out,
    tokens_out,
    cotangent_out,
    wide,
    down,
    rows_in,
    cot,
    cot_own,
    cot_pair,
    exact,
    packed,
    first,
    merged,
    from_left,
    from_right,
    z_send,
    z_recv,
    saved,
    whole,
    core_send,
    core_recv,
    y_exact,
    y_packed,
    y_first,
    y_merged,
    y_left,
    y_right,
    dp_send,
    dp_recv,
    swap_send,
    swap_recv,
    result,
    send_sems,
    recv_sems,
    local_sems,
):
    dp, row, col = lax.axis_index("dp"), lax.axis_index("row"), lax.axis_index("col")
    x, zh, y, c = row // 2, row % 2, col // 2, col % 2
    x_right = (dp, lax.rem(x + 1, 4) * 2 + zh, col)
    x_left = (dp, lax.rem(x + 3, 4) * 2 + zh, col)
    y_next = (dp, row, lax.rem(y + 1, 4) * 2 + c)
    y_prev = (dp, row, lax.rem(y + 3, 4) * 2 + c)
    z_far = (dp, x * 2 + (1 - zh), col)
    z_near = (1 - dp, row, col)
    sibling = (dp, row, y * 2 + (1 - c))
    half_rows = rows_in.shape[2]
    block = half_rows // 4
    features = rows_in.shape[3]
    half_features = features // 2
    quarter = half_features // 2
    own_cols = pl.ds(pl.multiple_of(c * half_features, 128), half_features)
    other_cols = pl.ds(pl.multiple_of((1 - c) * half_features, 128), half_features)
    cp = Copies(send_sems, recv_sems, local_sems)

    load_tokens = cp.local(tokens, rows_in.at[0, 0])
    load_cot = cp.local(cotangent, cot_own)
    load_wide = [cp.local(gate_weight, wide.at[0]), cp.local(up_weight, wide.at[1])]
    load_tangent = cp.local(token_tangent, rows_in.at[0, 1])
    load_wide += [cp.local(gate_delta, wide.at[2]), cp.local(up_delta, wide.at[3])]
    load_down = [cp.local(down_weight, down.at[0]), cp.local(down_delta, down.at[1])]

    barrier = pltpu.get_barrier_semaphore()
    partners = (x_right, x_left, y_next, y_prev, z_far, z_near, sibling)
    for device in partners:
        pl.semaphore_signal(barrier, inc=1, device_id=device, device_id_type=MESH)
    pl.semaphore_wait(barrier, len(partners))

    my_part = pl.ds(pl.multiple_of(c * (half_rows // 2), 16), half_rows // 2)

    def send_rows(which):
        return cp.start(rows_in.at[0, which, my_part], rows_in.at[1, which, my_part], z_near)

    def forward_rows(which):
        return cp.start(rows_in.at[1, which, my_part], rows_in.at[1, which, my_part], sibling)

    load_tokens.wait()
    rows_a = send_rows(0)

    small = block // 2
    load_cot.wait()
    my_small = pl.ds(pl.multiple_of(c * small, 8), small)
    cot_pair[my_small] = cot_own[...].astype(F32)
    pair_copy = cp.start(cot_pair.at[my_small], cot_pair.at[my_small], sibling)

    def y_rows(shift):
        return pl.ds(pl.multiple_of(lax.rem(y + shift, 4) * block, 16), block)

    def cot_send(shift, device, cols):
        part = cot.at[0, y_rows(shift), cols]
        return cp.start(part, part, device)

    ring = []
    for unit in range(5):
        ring.append(
            RingSum(
                cp, x, x_left, x_right, block, exact.at[unit], packed.at[unit], first.at[unit],
                merged.at[unit], from_left.at[unit], from_right.at[unit],
            )
        )
    gathers = [RingGather(cp, x, x_left, x_right, block, whole.at[k]) for k in range(4)]

    def store_partial(unit, plane, value):
        exact[unit, plane] = value
        packed[unit, plane] = value.astype(BF16)

    def forward_sums(unit, half):
        for plane in range(2):
            store_partial(unit, plane, dot(rows_in[half, 0], wide[plane]))

    def forward_tangents(unit, half):
        for plane in range(2):
            store_partial(
                unit,
                plane,
                dot(rows_in[half, 0], wide[2 + plane]) + dot(rows_in[half, 1], wide[plane]),
            )

    z_copies = {}

    def finish_x(unit):
        ring[unit].wait()
        for plane in range(2):
            value = ring[unit].total(plane)
            exact[unit, plane, ring[unit].rows(0)] = value
            z_send[unit, plane] = value.astype(z_send.dtype)
        z_copies[unit] = cp.start(z_send.at[unit], z_recv.at[unit], z_far)

    def total(unit, plane):
        return exact[unit, plane, ring[unit].rows(0)] + z_recv[unit, plane].astype(F32)

    def hidden_block(half):
        sums, tangents = 2 * half, 2 * half + 1
        gate_sum, up_sum = total(sums, 0), total(sums, 1)
        gate_tangent, up_tangent = total(tangents, 0), total(tangents, 1)
        logistic = jax.nn.sigmoid(gate_sum)
        activation = gate_sum * logistic
        derivative = logistic * (1.0 + gate_sum * (1.0 - logistic))
        mine = gathers[half].rows(0)
        whole[half, 0, mine] = (activation * up_sum).astype(BF16)
        whole[half, 1, mine] = (
            derivative * gate_tangent * up_sum + activation * up_tangent
        ).astype(BF16)
        saved[half, 0] = up_sum * derivative
        saved[half, 1] = activation
        gathers[half].start()

    def grad_block(half):
        back = total(4, half)
        mine = gathers[2 + half].rows(0)
        whole[2 + half, 0, mine] = (back * saved[half, 0]).astype(BF16)
        whole[2 + half, 1, mine] = (back * saved[half, 1]).astype(BF16)
        gathers[2 + half].start()

    widths = [half_features, half_features, quarter, quarter]
    out_ring, core_copies, dp_copies, swap_copies = {}, {}, {}, {}

    def unit_view(ref, unit):
        return ref.at[unit, :, :, pl.ds(0, widths[unit])]

    def output_part(unit, cols_start):
        half = unit % 2
        cols = pl.ds(pl.multiple_of(cols_start, 128), half_features)
        hidden, hidden_tangent = whole[half, 0], whole[half, 1]
        yield 0, dot(hidden, down[0, :, cols])
        yield 1, dot(hidden_tangent, down[0, :, cols]) + dot(hidden, down[1, :, cols])

    def input_part(unit, cols_start):
        half = unit % 2
        for plane in range(2):
            cols = pl.ds(pl.multiple_of(cols_start + plane * quarter, 128), quarter)
            yield (
                plane,
                dot_trans(whole[2 + half, 0], wide[0, cols])
                + dot_trans(whole[2 + half, 1], wide[1, cols]),
            )

    def out_compute(unit):
        width = widths[unit]
        part = output_part if unit < 2 else input_part
        for plane, value in part(unit, (1 - c) * half_features):
            core_send[unit, plane, :, 0:width] = value
        core_copies[unit] = cp.start(
            unit_view(core_send, unit), unit_view(core_recv, unit), sibling
        )
        for plane, value in part(unit, c * half_features):
            y_exact[unit, plane, :, 0:width] = value

    def out_start(unit):
        width = widths[unit]
        core_copies[unit].wait_recv()
        for plane in range(2):
            value = y_exact[unit, plane, :, 0:width] + core_recv[unit, plane, :, 0:width]
            y_exact[unit, plane, :, 0:width] = value
            y_packed[unit, plane, :, 0:width] = value.astype(BF16)
        views = [unit_view(r, unit) for r in (y_exact, y_packed, y_first, y_merged, y_left, y_right)]
        out_ring[unit] = RingSum(cp, y, y_prev, y_next, block, *views)
        out_ring[unit].start()

    def out_merge(unit):
        out_ring[unit].merge()

    def out_dp(unit):
        width = widths[unit]
        out_ring[unit].wait()
        slot = unit // 2
        for plane in range(2):
            dp_send[slot, plane, :, 0:width] = out_ring[unit].total(plane)
        cols = pl.ds(0, width)
        dp_copies[slot] = cp.start(
            dp_send.at[slot, :, :, cols], dp_recv.at[slot, :, :, cols], z_near
        )

    def out_swap(unit):
        width = widths[unit]
        out_ring[unit].wait()
        slot = unit // 2
        dp_copies[slot].wait_recv()
        for plane in range(2):
            swap_send[slot, plane, :, 0:width] = (
                out_ring[unit].total(plane) + dp_recv[slot, plane, :, 0:width]
            )
        theirs = pl.ds(pl.multiple_of((1 - c) * small, 8), small)
        cols = pl.ds(0, width)
        swap_copies[slot] = cp.start(
            swap_send.at[slot, :, theirs, cols], swap_recv.at[slot, :, :, cols], sibling
        )

    stores = []

    def out_store(unit):
        slot = unit // 2
        swap_copies[slot].wait_recv()
        width = widths[unit]
        for plane in range(2):
            mine = swap_send[slot, plane, my_small, 0:width].astype(BF16)
            other = swap_recv[slot, plane, :, 0:width].astype(BF16)
            if unit < 2:
                result[plane, :, own_cols] = mine
                result[plane, :, other_cols] = other
            else:
                shift = plane * quarter
                result[2, :, pl.ds(pl.multiple_of(c * half_features + shift, 128), width)] = mine
                result[2, :, pl.ds(pl.multiple_of((1 - c) * half_features + shift, 128), width)] = other
        if unit < 2:
            stores.append(cp.local(result.at[0], primal_out))
            stores.append(cp.local(result.at[1], tangent_out))
        else:
            stores.append(cp.local(result.at[2], input_out))

    load_wide[0].wait()
    load_wide[1].wait()
    load_tangent.wait()
    rows_b = send_rows(1)
    forward_sums(0, 0)
    ring[0].start()

    pair_copy.wait_recv()
    cot[0, y_rows(0)] = cot_pair[...].astype(BF16)
    cot_from_prev = cot_send(0, y_next, own_cols)
    cot_from_next = cot_send(0, y_prev, own_cols)

    load_wide[2].wait()
    load_wide[3].wait()
    forward_tangents(1, 0)
    ring[1].start()
    ring[0].merge()

    cot_from_prev.wait_recv()
    cot_far = cot_send(3, y_next, own_cols)
    rows_a.wait_recv()
    rows_c = forward_rows(0)
    cot_from_next.wait_recv()
    cot_far.wait_recv()
    cot_dp = cp.start(cot.at[0, :, own_cols], cot.at[1, :, own_cols], z_near)
    cot_siblings = [cot_send(shift, sibling, own_cols) for shift in (1, 2, 3)]
    rows_c.wait_recv()
    forward_sums(2, 1)
    ring[2].start()
    ring[1].merge()
    finish_x(0)
    rows_b.wait_recv()
    rows_d = forward_rows(1)
    rows_d.wait_recv()
    forward_tangents(3, 1)
    ring[3].start()
    ring[2].merge()
    finish_x(1)

    cot_dp.wait_recv()
    cot_last = cp.start(cot.at[1, :, own_cols], cot.at[1, :, own_cols], sibling)
    for copy in cot_siblings:
        copy.wait_recv()
    load_down[0].wait()
    store_partial(4, 0, dot_trans(cot[0], down[0]))
    cot_last.wait_recv()
    store_partial(4, 1, dot_trans(cot[1], down[0]))
    ring[4].start()
    ring[3].merge()
    z_copies[0].wait_recv()
    z_copies[1].wait_recv()
    hidden_block(0)
    for half in range(2):
        stores.append(cp.local(rows_in.at[half, 0], tokens_out.at[half]))
        stores.append(cp.local(cot.at[half], cotangent_out.at[half]))
    finish_x(2)
    ring[4].merge()
    finish_x(3)
    gathers[0].forward()
    z_copies[2].wait_recv()
    z_copies[3].wait_recv()
    hidden_block(1)
    finish_x(4)
    gathers[0].wait()
    stores.append(cp.local(whole.at[0, 0], hidden_out.at[0]))
    z_copies[4].wait_recv()
    grad_block(1)
    grad_block(0)
    load_down[1].wait()
    out_compute(0)
    gathers[1].forward()
    out_start(0)
    gathers[1].wait()
    stores.append(cp.local(whole.at[1, 0], hidden_out.at[1]))
    out_compute(1)
    gathers[3].forward()
    out_merge(0)
    out_start(1)
    gathers[2].forward()
    out_merge(1)
    gathers[3].wait()
    stores.append(cp.local(whole.at[3, 0], grad_gate_out.at[1]))
    stores.append(cp.local(whole.at[3, 1], grad_up_out.at[1]))
    out_compute(3)
    out_start(3)
    out_dp(1)
    gathers[2].wait()
    stores.append(cp.local(whole.at[2, 0], grad_gate_out.at[0]))
    stores.append(cp.local(whole.at[2, 1], grad_up_out.at[0]))
    out_compute(2)
    out_start(2)
    out_merge(3)
    out_swap(0)
    out_merge(2)
    out_dp(3)
    out_store(0)
    out_swap(2)
    out_store(2)

    for copy in cp.sent:
        copy.wait_send()
    for copy in stores:
        copy.wait()


def gradient_kernel(normalizer, tokens, cotangent, hidden, grad_gate, grad_up, gate_out, up_out, down_out):
    gate_out[...] = (
        lax.dot_general(tokens[...], grad_gate[...], TRANS_LEFT, preferred_element_type=F32)
        * normalizer
    ).astype(BF16)
    up_out[...] = (
        lax.dot_general(tokens[...], grad_up[...], TRANS_LEFT, preferred_element_type=F32)
        * normalizer
    ).astype(BF16)
    down_out[...] = (
        lax.dot_general(hidden[...], cotangent[...], TRANS_LEFT, preferred_element_type=F32)
        * normalizer
    ).astype(BF16)


def on_device(*arguments):
    tokens, _, gate_weight, _, _, _, _, _, cotangent = arguments
    half_rows, features = tokens.shape
    units = gate_weight.shape[1]
    block = half_rows // 4
    half_features = features // 2
    small = cotangent.shape[0]
    shape = jax.ShapeDtypeStruct
    hbm = pl.BlockSpec(memory_space=pl.ANY)
    vm = pltpu.VMEM
    outs = pl.pallas_call(
        main_kernel,
        out_shape=[shape((small, features), BF16)] * 3
        + [shape((2, half_rows, units), BF16)] * 3
        + [shape((2, half_rows, features), BF16)] * 2,
        in_specs=[hbm] * 9,
        out_specs=[hbm] * 8,
        scratch_shapes=[
            vm((4, features, units), BF16),
            vm((2, units, features), BF16),
            vm((2, 2, half_rows, features), BF16),
            vm((2, half_rows, features), BF16),
            vm((small, features), BF16),
            vm((block, features), F32),
            vm((5, 2, half_rows, units), F32),
            vm((5, 2, half_rows, units), BF16),
            vm((5, 2, block, units), BF16),
            vm((5, 2, block, units), BF16),
            vm((5, 2, block, units), BF16),
            vm((5, 2, block, units), BF16),
            vm((5, 2, block, units), BF16),
            vm((5, 2, block, units), BF16),
            vm((2, 2, block, units), F32),
            vm((4, 2, half_rows, units), BF16),
            vm((4, 2, half_rows, half_features), F32),
            vm((4, 2, half_rows, half_features), F32),
            vm((4, 2, half_rows, half_features), F32),
            vm((4, 2, half_rows, half_features), BF16),
            vm((4, 2, block, half_features), BF16),
            vm((4, 2, block, half_features), BF16),
            vm((4, 2, block, half_features), BF16),
            vm((4, 2, block, half_features), BF16),
            vm((2, 2, block, half_features), F32),
            vm((2, 2, block, half_features), F32),
            vm((2, 2, block, half_features), F32),
            vm((2, 2, small, half_features), F32),
            vm((3, small, features), BF16),
            pltpu.SemaphoreType.DMA((120,)),
            pltpu.SemaphoreType.DMA((120,)),
            pltpu.SemaphoreType.DMA((32,)),
        ],
        compiler_params=pltpu.CompilerParams(
            collective_id=0, has_side_effects=True, vmem_limit_bytes=60 << 20
        ),
        cost_estimate=pl.CostEstimate(
            flops=24 * 2 * half_rows * features * units,
            bytes_accessed=12 * features * units,
            transcendentals=0,
        ),
        name="linearized_block",
    )(*arguments)
    primal, tangent, input_cotangent, hidden, grad_gate, grad_up, rows_in, cot = outs
    flat = lambda value: value.reshape(2 * half_rows, value.shape[2])
    vmem = pl.BlockSpec(memory_space=pltpu.VMEM)
    normalizer = 1.0 / math.sqrt(2 * half_rows)
    gate_gradient, up_gradient, down_gradient = pl.pallas_call(
        functools.partial(gradient_kernel, normalizer),
        out_shape=[shape((features, units), BF16)] * 2 + [shape((units, features), BF16)],
        in_specs=[vmem] * 5,
        out_specs=[vmem] * 3,
        compiler_params=pltpu.CompilerParams(vmem_limit_bytes=60 << 20),
        cost_estimate=pl.CostEstimate(
            flops=6 * 2 * half_rows * features * units,
            bytes_accessed=6 * features * units + 16 * half_rows * features,
            transcendentals=0,
        ),
        name="gradients",
    )(flat(rows_in), flat(cot), flat(hidden), flat(grad_gate), flat(grad_up))
    return (primal, tangent, input_cotangent, gate_gradient, up_gradient, down_gradient)


def solution(mesh):
    by_dp = P("dp", "row")
    wide = P("row", ("dp", "col"))
    tall = P(("dp", "col"), "row")
    return jax.shard_map(
        on_device,
        mesh=mesh,
        in_specs=(by_dp, by_dp, wide, wide, wide, wide, tall, tall, tall),
        out_specs=(tall, tall, tall, wide, wide, tall),
        check_vma=False,
    )
```

time: 504 us -> 95.1 us (0.19)
  waiting for transfers between devices: 389 us -> 0 us
  Pallas kernels: 0 us -> 92.5 us
  blocking collectives: 46.5 us -> 0 us
  matrix products: 31 us -> 0 us
  between operations: 13.9 us -> 0.67 us
  local copies, waits for them, and re-layouts: 10.3 us -> 1.87 us
  other arithmetic: 8.37 us -> 0 us
    psum x1 -> x0, waiting for transfers between devices: 288 us -> none  [forward_block(): lax.psum((partials[0], partials[1], partials[2], partials[3]), 'row')]
    reduce_scatter x2 -> x0, waiting for transfers between devices: 102 us -> none  [the longest x1 64.6 us: on_device(): lax.psum_scatter(jnp.concatenate((primal, tangent), axis=1), ('dp', 'col'...]
    pallas_call x0 -> x2, Pallas kernels: none -> 92.5 us  [the longest x1 85.8 us: on_device(): pl.pallas_call(main_kernel, out_shape=[shape((small, features), BF16)] *...]
    all_gather x3 -> x0, blocking collectives: 46.5 us -> none  [the longest x1 23.9 us: on_device(): lax.all_gather(cotangent, ('dp', 'col'), axis=0, tiled=True)]
    dot_general x15 -> x0, matrix products: 31 us -> none  [the longest x9 16.3 us: matmul(): return jnp.dot(left_side, right_side, preferred_element_type=jnp.float32)]
    unnamed x36 -> x9, local copies, waits for them, and re-layouts: 9.69 us -> 1.87 us
    convert_element_type x2 -> x0, other arithmetic: 5.43 us -> none  [the longest x1 3.91 us: backward_block(): grad_up = (back_sum * activation).astype(jnp.bfloat16)]
  transfers between devices with their start and end apart: 3 -> 0, of which waited for: 3 -> 0; matrix products, arithmetic and copies ran while one was open for 5% -> 0% of each run, Pallas kernels for 0% -> 0%
where the time goes in v1:
time: 95.1 us; the launch traced here: 95 us
  Pallas kernels  92.5 us (97%)
  local copies, waits for them, and re-layouts  1.87 us (2%)
    pallas_call x1, Pallas kernels, on_device(): pl.pallas_call(main_kernel, out_shape=[shape((small, features), BF16)] *...  85.8 us
    pallas_call x1, Pallas kernels, on_device(): pl.pallas_call(functools.partial(gradient_kernel, normalizer), out_shape=...  6.64 us

profile of v1, /device:TPU:1, one launch (start us, length us, event | category | flops | bytes accessed | tf_op | source)
XLA Modules:
  0.0 95.0 jit_solution(13871484297560240822)
XLA Ops:
  0.6 85.8 %linearized_block.1 = (bf16[24,1024]{1,0:T(8,128)(2,1)}, bf16[24,1024]{1,0:T(8,128)(2,1)}, bf16[24,1024]{1,0:T(8,128)(2,1)}, bf16[2,192,896]{2,1,0:T(8,128)(2,1)...) custom-call(bf16[192,1024]{1,0:T(8,128)(2,1)} %tokens.1, ...), custom_call_target="tpu_custom_call" | custom-call | flops 8455716864 | bytes 11010048 | tf_op jit(solution)/shard_map/linearized_block/pallas_call | solution.py:512
  86.5 0.0 copy-start.2
  86.5 0.0 copy-start.1
  86.5 0.0 copy-start
  86.5 6.6 %gradients.1 = (bf16[1024,896]{1,0:T(8,128)(2,1)}, bf16[1024,896]{1,0:T(8,128)(2,1)}, bf16[896,1024]{1,0:T(8,128)(2,1)}) custom-call(bf16[384,1024]{1,0:T(8,128)(2,1)} %bitcast.5, bf16[384,1024]{1,0:T(8,128)(2,1)} %bitcast.6, bf16[384,896]{1,0:T(8,128)(2,1)} %bitcast.7, bf16[384,896]{1,0:T(8,128)(2,1)} %bitcast.8, bf16[384,896]{1,0:T(8,128)(2,1)} %bitcast.9), custom_call_target="tpu_custom_call" | custom-call | flops 2113929216 | bytes 8650752 | tf_op jit(solution)/shard_map/gradients/pallas_call | solution.py:567
  93.1 0.0 copy-done.2
  93.1 0.6 copy.18
  93.8 0.0 copy-done.1
  93.8 0.6 copy.19
  94.4 0.0 copy-done
  94.4 0.6 copy.20
Async XLA Ops:
  86.5 6.7 %copy-start.2 = (bf16[24,1024]{1,0:T(8,128)(2,1)S(1)}, bf16[24,1024]{1,0:T(8,128)(2,1)}, u32[]{:S(2)}) copy-start(bf16[24,1024]{1,0:T(8,128)(2,1)} %get-tuple-element.34) | copy-start | bytes 147460
  86.5 7.3 %copy-start.1 = (bf16[24,1024]{1,0:T(8,128)(2,1)S(1)}, bf16[24,1024]{1,0:T(8,128)(2,1)}, u32[]{:S(2)}) copy-start(bf16[24,1024]{1,0:T(8,128)(2,1)} %get-tuple-element.35) | copy-start | bytes 147460
  86.5 7.9 %copy-start = (bf16[24,1024]{1,0:T(8,128)(2,1)S(1)}, bf16[24,1024]{1,0:T(8,128)(2,1)}, u32[]{:S(2)}) copy-start(bf16[24,1024]{1,0:T(8,128)(2,1)} %get-tuple-element.36) | copy-start | bytes 147460

commit v2 on v1

--- a/solution.py
+++ b/solution.py
@@ -71,10 +71,10 @@
     def merge(self):
         send = self.copies.start
         self.a0.wait_recv()
-        self.merged[0] = (self.exact[0, self.rows(1)] + self.first[0].astype(F32)).astype(BF16)
+        self.merged[0] = (self.exact[0, self.rows(1)] + self.first[0].astype(F32)).astype(self.merged.dtype)
         self.c0 = send(self.merged.at[0], self.from_left.at[0], self.right)
         self.a1.wait_recv()
-        self.merged[1] = (self.exact[1, self.rows(3)] + self.first[1].astype(F32)).astype(BF16)
+        self.merged[1] = (self.exact[1, self.rows(3)] + self.first[1].astype(F32)).astype(self.merged.dtype)
         self.c1 = send(self.merged.at[1], self.from_right.at[1], self.left)
 
     def wait(self):
@@ -112,6 +112,79 @@
 
     def wait(self):
         for copy in (self.b0, self.b1, self.c0, self.c1):
+            copy.wait_recv()
+
+
+class SplitGather:
+    def __init__(self, copies, me, left, right, block, split, whole):
+        self.copies, self.left, self.right, self.whole = copies, left, right, whole
+        units = whole.shape[1]
+        self.parts = (pl.ds(0, split), pl.ds(split, units - split))
+        self.rows = lambda shift: pl.ds(pl.multiple_of(lax.rem(me + shift, 4) * block, 16), block)
+
+    def send(self, part, shift, device):
+        view = self.whole.at[self.rows(shift), self.parts[part]]
+        return self.copies.start(view, view, device)
+
+    def start(self):
+        self.a0 = self.send(0, 0, self.right)
+        self.a1 = self.send(1, 0, self.left)
+        self.b1 = self.send(1, 0, self.right)
+        self.b0 = self.send(0, 0, self.left)
+
+    def forward(self):
+        self.a0.wait_recv()
+        self.c0 = self.send(0, 3, self.right)
+        self.a1.wait_recv()
+        self.c1 = self.send(1, 1, self.left)
+
+    def wait(self):
+        for copy in (self.b0, self.b1, self.c0, self.c1):
+            copy.wait_recv()
+
+
+class PlaneGather:
+    def __init__(self, copies, me, left, right, far, plane, block, split, whole):
+        self.copies, self.left, self.right, self.far = copies, left, right, far
+        self.plane, self.whole = plane, whole
+        units = whole.shape[2]
+        self.parts = (pl.ds(0, split), pl.ds(split, units - split))
+        self.rows = lambda shift: pl.ds(pl.multiple_of(lax.rem(me + shift, 4) * block, 16), block)
+        self.crossed = []
+
+    def send(self, part, shift, device):
+        view = self.whole.at[self.plane, self.rows(shift), self.parts[part]]
+        return self.copies.start(view, view, device)
+
+    def cross(self, part, shift):
+        self.crossed.append(self.send(part, shift, self.far))
+
+    def start(self):
+        self.a0 = self.send(0, 0, self.right)
+        self.a1 = self.send(1, 0, self.left)
+        self.b1 = self.send(1, 0, self.right)
+        self.b0 = self.send(0, 0, self.left)
+
+    def forward(self):
+        self.a0.wait_recv()
+        self.c0 = self.send(0, 3, self.right)
+        self.cross(0, 3)
+        self.a1.wait_recv()
+        self.c1 = self.send(1, 1, self.left)
+        self.cross(1, 1)
+
+    def forward_far(self):
+        self.b1.wait_recv()
+        self.cross(1, 3)
+        self.b0.wait_recv()
+        self.cross(0, 1)
+        self.c0.wait_recv()
+        self.cross(0, 2)
+        self.c1.wait_recv()
+        self.cross(1, 2)
+
+    def wait(self):
+        for copy in self.crossed:
             copy.wait_recv()
 
 
@@ -147,21 +220,35 @@
     from_right,
     z_send,
     z_recv,
+    z_wide_send,
+    z_wide_recv,
     saved,
     whole,
     core_send,
     core_recv,
     y_exact,
-    y_packed,
     y_first,
     y_merged,
     y_left,
     y_right,
+    y_packed,
+    p_first,
+    p_merged,
+    p_left,
+    p_right,
+    in_packed,
+    in_first,
+    in_merged,
+    in_left,
+    in_right,
     dp_send,
     dp_recv,
     swap_send,
     swap_recv,
     result,
+    tokens_turned,
+    hidden_turned,
+    tangent_base,
     send_sems,
     recv_sems,
     local_sems,
@@ -217,9 +304,14 @@
     def y_rows(shift):
         return pl.ds(pl.multiple_of(lax.rem(y + shift, 4) * block, 16), block)
 
-    def cot_send(shift, device, cols):
-        part = cot.at[0, y_rows(shift), cols]
+    def cot_send(half, shift, device):
+        part = cot.at[half, y_rows(shift), own_cols]
         return cp.start(part, part, device)
+
+    def cot_over_dp():
+        return cp.start(
+            cot.at[0, y_rows(0), own_cols], cot.at[1, y_rows(0), own_cols], z_near
+        )
 
     ring = []
     for unit in range(5):
@@ -229,7 +321,15 @@
                 merged.at[unit], from_left.at[unit], from_right.at[unit],
             )
         )
-    gathers = [RingGather(cp, x, x_left, x_right, block, whole.at[k]) for k in range(4)]
+    split = (whole.shape[3] // 2 + 127) // 128 * 128
+    hidden_gather = RingGather(cp, x, x_left, x_right, block, whole.at[0])
+    tangent_gather = [
+        SplitGather(cp, x, x_left, x_right, block, split, whole.at[1, half]) for half in range(2)
+    ]
+    grad_gather = [
+        RingGather(cp, x, x_left, x_right, block, whole.at[2]),
+        PlaneGather(cp, x, x_left, x_right, z_far, zh, block, split, whole.at[3]),
+    ]
 
     def store_partial(unit, plane, value):
         exact[unit, plane] = value
@@ -254,34 +354,39 @@
         for plane in range(2):
             value = ring[unit].total(plane)
             exact[unit, plane, ring[unit].rows(0)] = value
-            z_send[unit, plane] = value.astype(z_send.dtype)
-        z_copies[unit] = cp.start(z_send.at[unit], z_recv.at[unit], z_far)
+            z_refs(unit)[0][plane] = value.astype(z_refs(unit)[0].dtype)
+        z_copies[unit] = cp.start(*z_refs(unit), z_far)
+
+    def z_refs(unit):
+        if unit in (0, 2):
+            return z_wide_send.at[unit // 2], z_wide_recv.at[unit // 2]
+        return z_send.at[unit], z_recv.at[unit]
 
     def total(unit, plane):
-        return exact[unit, plane, ring[unit].rows(0)] + z_recv[unit, plane].astype(F32)
+        return exact[unit, plane, ring[unit].rows(0)] + z_refs(unit)[1][plane].astype(F32)
 
     def hidden_block(half):
-        sums, tangents = 2 * half, 2 * half + 1
-        gate_sum, up_sum = total(sums, 0), total(sums, 1)
-        gate_tangent, up_tangent = total(tangents, 0), total(tangents, 1)
+        gate_sum, up_sum = total(2 * half, 0), total(2 * half, 1)
         logistic = jax.nn.sigmoid(gate_sum)
         activation = gate_sum * logistic
         derivative = logistic * (1.0 + gate_sum * (1.0 - logistic))
-        mine = gathers[half].rows(0)
-        whole[half, 0, mine] = (activation * up_sum).astype(BF16)
-        whole[half, 1, mine] = (
-            derivative * gate_tangent * up_sum + activation * up_tangent
-        ).astype(BF16)
+        whole[0, half, ring[0].rows(0)] = (activation * up_sum).astype(BF16)
         saved[half, 0] = up_sum * derivative
         saved[half, 1] = activation
-        gathers[half].start()
+
+    def tangent_block(half):
+        unit = 2 * half + 1
+        whole[1, half, ring[0].rows(0)] = (
+            saved[half, 0] * total(unit, 0) + saved[half, 1] * total(unit, 1)
+        ).astype(BF16)
+        tangent_gather[half].start()
 
     def grad_block(half):
         back = total(4, half)
-        mine = gathers[2 + half].rows(0)
+        mine = ring[0].rows(0)
         whole[2 + half, 0, mine] = (back * saved[half, 0]).astype(BF16)
         whole[2 + half, 1, mine] = (back * saved[half, 1]).astype(BF16)
-        gathers[2 + half].start()
+        grad_gather[half].start()
 
     widths = [half_features, half_features, quarter, quarter]
     out_ring, core_copies, dp_copies, swap_copies = {}, {}, {}, {}
@@ -289,32 +394,40 @@
     def unit_view(ref, unit):
         return ref.at[unit, :, :, pl.ds(0, widths[unit])]
 
-    def output_part(unit, cols_start):
-        half = unit % 2
-        cols = pl.ds(pl.multiple_of(cols_start, 128), half_features)
-        hidden, hidden_tangent = whole[half, 0], whole[half, 1]
-        yield 0, dot(hidden, down[0, :, cols])
-        yield 1, dot(hidden_tangent, down[0, :, cols]) + dot(hidden, down[1, :, cols])
-
-    def input_part(unit, cols_start):
-        half = unit % 2
+    def columns(start, width):
+        return pl.ds(pl.multiple_of(start, 128), width)
+
+    def out_part(unit, start):
+        width = widths[unit]
         for plane in range(2):
-            cols = pl.ds(pl.multiple_of(cols_start + plane * quarter, 128), quarter)
-            yield (
-                plane,
-                dot_trans(whole[2 + half, 0], wide[0, cols])
-                + dot_trans(whole[2 + half, 1], wide[1, cols]),
-            )
+            if unit == 0:
+                yield plane, dot(whole[0, plane], down[0, :, columns(start, width)])
+            elif unit == 1:
+                rows = columns(start, width)
+                yield (
+                    plane,
+                    dot_trans(whole[2 + plane, 0], wide[0, rows])
+                    + dot_trans(whole[2 + plane, 1], wide[1, rows]),
+                )
+            else:
+                half = unit - 2
+                cols = columns(start + plane * width, width)
+                yield (
+                    plane,
+                    dot(whole[1, half], down[0, :, cols]) + tangent_base[half, :, cols],
+                )
+
+    def base_compute(half):
+        tangent_base[half] = dot(whole[0, half], down[1])
 
     def out_compute(unit):
         width = widths[unit]
-        part = output_part if unit < 2 else input_part
-        for plane, value in part(unit, (1 - c) * half_features):
+        for plane, value in out_part(unit, (1 - c) * half_features):
             core_send[unit, plane, :, 0:width] = value
         core_copies[unit] = cp.start(
             unit_view(core_send, unit), unit_view(core_recv, unit), sibling
         )
-        for plane, value in part(unit, c * half_features):
+        for plane, value in out_part(unit, c * half_features):
             y_exact[unit, plane, :, 0:width] = value
 
     def out_start(unit):
@@ -323,9 +436,20 @@
         for plane in range(2):
             value = y_exact[unit, plane, :, 0:width] + core_recv[unit, plane, :, 0:width]
             y_exact[unit, plane, :, 0:width] = value
-            y_packed[unit, plane, :, 0:width] = value.astype(BF16)
-        views = [unit_view(r, unit) for r in (y_exact, y_packed, y_first, y_merged, y_left, y_right)]
-        out_ring[unit] = RingSum(cp, y, y_prev, y_next, block, *views)
+            if unit == 1:
+                y_packed[plane] = value.astype(BF16)
+            if unit >= 2:
+                in_packed[unit - 2, plane] = value.astype(BF16)
+        summed = unit_view(y_exact, unit)
+        if unit == 0:
+            views = [summed, y_first, y_merged, y_left, y_right]
+        elif unit == 1:
+            views = [y_packed, p_first, p_merged, p_left, p_right]
+        else:
+            views = [
+                r.at[unit - 2] for r in (in_packed, in_first, in_merged, in_left, in_right)
+            ]
+        out_ring[unit] = RingSum(cp, y, y_prev, y_next, block, summed, *views)
         out_ring[unit].start()
 
     def out_merge(unit):
@@ -333,149 +457,161 @@
 
     def out_dp(unit):
         width = widths[unit]
+        slot = min(unit, 2)
         out_ring[unit].wait()
-        slot = unit // 2
-        for plane in range(2):
+        planes = (1,) if unit < 2 else (0, 1)
+        for plane in planes:
             dp_send[slot, plane, :, 0:width] = out_ring[unit].total(plane)
+        part = pl.ds(planes[0], len(planes))
         cols = pl.ds(0, width)
         dp_copies[slot] = cp.start(
-            dp_send.at[slot, :, :, cols], dp_recv.at[slot, :, :, cols], z_near
+            dp_send.at[slot, part, :, cols], dp_recv.at[slot, part, :, cols], z_near
         )
+
+    theirs = pl.ds(pl.multiple_of((1 - c) * small, 8), small)
 
     def out_swap(unit):
         width = widths[unit]
-        out_ring[unit].wait()
-        slot = unit // 2
-        dp_copies[slot].wait_recv()
-        for plane in range(2):
-            swap_send[slot, plane, :, 0:width] = (
-                out_ring[unit].total(plane) + dp_recv[slot, plane, :, 0:width]
+        if unit == 2:
+            out_ring[unit].wait()
+        dp_copies[unit].wait_recv()
+        planes = (0,) if unit < 2 else (0, 1)
+        for plane in planes:
+            swap_send[unit, plane, :, 0:width] = (
+                out_ring[unit].total(plane)
+                + dp_recv[unit, 1 if unit < 2 else plane, :, 0:width]
             )
-        theirs = pl.ds(pl.multiple_of((1 - c) * small, 8), small)
+        part = pl.ds(0, len(planes))
         cols = pl.ds(0, width)
-        swap_copies[slot] = cp.start(
-            swap_send.at[slot, :, theirs, cols], swap_recv.at[slot, :, :, cols], sibling
+        swap_copies[unit] = cp.start(
+            swap_send.at[unit, part, theirs, cols], swap_recv.at[unit, part, :, cols], sibling
         )
 
     stores = []
 
     def out_store(unit):
-        slot = unit // 2
-        swap_copies[slot].wait_recv()
+        swap_copies[unit].wait_recv()
         width = widths[unit]
-        for plane in range(2):
-            mine = swap_send[slot, plane, my_small, 0:width].astype(BF16)
-            other = swap_recv[slot, plane, :, 0:width].astype(BF16)
-            if unit < 2:
-                result[plane, :, own_cols] = mine
-                result[plane, :, other_cols] = other
-            else:
-                shift = plane * quarter
-                result[2, :, pl.ds(pl.multiple_of(c * half_features + shift, 128), width)] = mine
-                result[2, :, pl.ds(pl.multiple_of((1 - c) * half_features + shift, 128), width)] = other
-        if unit < 2:
-            stores.append(cp.local(result.at[0], primal_out))
-            stores.append(cp.local(result.at[1], tangent_out))
-        else:
-            stores.append(cp.local(result.at[2], input_out))
+        for plane in range(1 if unit < 2 else 2):
+            mine = columns(c * half_features + plane * width, width)
+            other = columns((1 - c) * half_features + plane * width, width)
+            result[unit, :, mine] = swap_send[unit, plane, my_small, 0:width].astype(BF16)
+            result[unit, :, other] = swap_recv[unit, plane, :, 0:width].astype(BF16)
+        outs = (primal_out, input_out, tangent_out)
+        stores.append(cp.local(result.at[unit], outs[unit]))
 
     load_wide[0].wait()
     load_wide[1].wait()
-    load_tangent.wait()
-    rows_b = send_rows(1)
     forward_sums(0, 0)
     ring[0].start()
 
     pair_copy.wait_recv()
     cot[0, y_rows(0)] = cot_pair[...].astype(BF16)
-    cot_from_prev = cot_send(0, y_next, own_cols)
-    cot_from_next = cot_send(0, y_prev, own_cols)
-
+    cot_cross = cot_over_dp()
+    cot_next = [cot_send(0, 0, y_next)]
+    cot_prev = [cot_send(0, 0, y_prev)]
+
+    load_tangent.wait()
     load_wide[2].wait()
     load_wide[3].wait()
     forward_tangents(1, 0)
     ring[1].start()
+    rows_b = send_rows(1)
     ring[0].merge()
-
-    cot_from_prev.wait_recv()
-    cot_far = cot_send(3, y_next, own_cols)
     rows_a.wait_recv()
     rows_c = forward_rows(0)
-    cot_from_next.wait_recv()
-    cot_far.wait_recv()
-    cot_dp = cp.start(cot.at[0, :, own_cols], cot.at[1, :, own_cols], z_near)
-    cot_siblings = [cot_send(shift, sibling, own_cols) for shift in (1, 2, 3)]
+    cot_next[0].wait_recv()
+    cot_far = [cot_send(0, 3, y_next)]
+    cot_cross.wait_recv()
+    cot_next.append(cot_send(1, 0, y_next))
+    cot_prev.append(cot_send(1, 0, y_prev))
+    cot_prev[0].wait_recv()
     rows_c.wait_recv()
     forward_sums(2, 1)
     ring[2].start()
     ring[1].merge()
+    cot_far[0].wait_recv()
+    cot_siblings = [cot_send(0, shift, sibling) for shift in (1, 2, 3)]
+    cot_next[1].wait_recv()
+    cot_far.append(cot_send(1, 3, y_next))
     finish_x(0)
-    rows_b.wait_recv()
-    rows_d = forward_rows(1)
-    rows_d.wait_recv()
-    forward_tangents(3, 1)
-    ring[3].start()
-    ring[2].merge()
-    finish_x(1)
-
-    cot_dp.wait_recv()
-    cot_last = cp.start(cot.at[1, :, own_cols], cot.at[1, :, own_cols], sibling)
     for copy in cot_siblings:
         copy.wait_recv()
     load_down[0].wait()
     store_partial(4, 0, dot_trans(cot[0], down[0]))
+    rows_b.wait_recv()
+    rows_d = forward_rows(1)
+    cot_prev[1].wait_recv()
+    cot_far[1].wait_recv()
+    cot_last = cp.start(cot.at[1, :, own_cols], cot.at[1, :, own_cols], sibling)
+    ring[2].merge()
     cot_last.wait_recv()
     store_partial(4, 1, dot_trans(cot[1], down[0]))
     ring[4].start()
-    ring[3].merge()
-    z_copies[0].wait_recv()
-    z_copies[1].wait_recv()
-    hidden_block(0)
-    for half in range(2):
-        stores.append(cp.local(rows_in.at[half, 0], tokens_out.at[half]))
-        stores.append(cp.local(cot.at[half], cotangent_out.at[half]))
+    rows_d.wait_recv()
+    forward_tangents(3, 1)
+    ring[3].start()
     finish_x(2)
     ring[4].merge()
+    z_copies[0].wait_recv()
+    hidden_block(0)
+    tokens_turned[...] = rows_in[:, 0].reshape(2 * half_rows, features).T
+    stores.append(cp.local(tokens_turned, tokens_out))
+    for half in range(2):
+        stores.append(cp.local(cot.at[half], cotangent_out.at[half]))
+    ring[3].merge()
+    finish_x(4)
     finish_x(3)
-    gathers[0].forward()
+    finish_x(1)
     z_copies[2].wait_recv()
-    z_copies[3].wait_recv()
     hidden_block(1)
-    finish_x(4)
-    gathers[0].wait()
-    stores.append(cp.local(whole.at[0, 0], hidden_out.at[0]))
+    hidden_gather.start()
+    hidden_gather.forward()
     z_copies[4].wait_recv()
     grad_block(1)
     grad_block(0)
+    z_copies[3].wait_recv()
+    tangent_block(1)
+    hidden_gather.wait()
+    grad_gather[1].forward()
     load_down[1].wait()
     out_compute(0)
-    gathers[1].forward()
+    z_copies[1].wait_recv()
+    tangent_block(0)
+    grad_gather[1].forward_far()
     out_start(0)
-    gathers[1].wait()
-    stores.append(cp.local(whole.at[1, 0], hidden_out.at[1]))
+    grad_gather[0].forward()
+    base_compute(0)
+    tangent_gather[1].forward()
+    base_compute(1)
+    out_merge(0)
+    tangent_gather[0].forward()
+    grad_gather[1].wait()
+    grad_gather[0].wait()
     out_compute(1)
-    gathers[3].forward()
-    out_merge(0)
+    out_dp(0)
+    tangent_gather[1].wait()
+    out_compute(3)
     out_start(1)
-    gathers[2].forward()
+    out_start(3)
+    tangent_gather[0].wait()
+    out_compute(2)
     out_merge(1)
-    gathers[3].wait()
-    stores.append(cp.local(whole.at[3, 0], grad_gate_out.at[1]))
-    stores.append(cp.local(whole.at[3, 1], grad_up_out.at[1]))
-    out_compute(3)
-    out_start(3)
-    out_dp(1)
-    gathers[2].wait()
-    stores.append(cp.local(whole.at[2, 0], grad_gate_out.at[0]))
-    stores.append(cp.local(whole.at[2, 1], grad_up_out.at[0]))
-    out_compute(2)
     out_start(2)
     out_merge(3)
-    out_swap(0)
+    hidden_turned[...] = whole[0].reshape(2 * half_rows, whole.shape[3]).T
+    stores.append(cp.local(hidden_turned, hidden_out))
+    out_dp(1)
     out_merge(2)
     out_dp(3)
+    out_swap(0)
+    for half in range(2):
+        stores.append(cp.local(whole.at[2 + half, 0], grad_gate_out.at[half]))
+        stores.append(cp.local(whole.at[2 + half, 1], grad_up_out.at[half]))
     out_store(0)
+    out_swap(1)
     out_swap(2)
+    out_store(1)
     out_store(2)
 
     for copy in cp.sent:
@@ -484,19 +620,70 @@
         copy.wait()
 
 
-def gradient_kernel(normalizer, tokens, cotangent, hidden, grad_gate, grad_up, gate_out, up_out, down_out):
-    gate_out[...] = (
-        lax.dot_general(tokens[...], grad_gate[...], TRANS_LEFT, preferred_element_type=F32)
-        * normalizer
-    ).astype(BF16)
-    up_out[...] = (
-        lax.dot_general(tokens[...], grad_up[...], TRANS_LEFT, preferred_element_type=F32)
-        * normalizer
-    ).astype(BF16)
-    down_out[...] = (
-        lax.dot_general(hidden[...], cotangent[...], TRANS_LEFT, preferred_element_type=F32)
-        * normalizer
-    ).astype(BF16)
+def gradient_kernel(
+    normalizer,
+    tokens,
+    hidden,
+    cotangent,
+    grad_gate,
+    grad_up,
+    primal,
+    tangent,
+    input_cotangent,
+    primal_out,
+    tangent_out,
+    input_out,
+    gate_out,
+    up_out,
+    down_out,
+    tokens_in,
+    hidden_in,
+    cotangent_in,
+    gate_in,
+    up_in,
+    small_in,
+    gate_rows,
+    up_rows,
+    down_rows,
+    sems,
+):
+    copies = []
+
+    def start(src, dst):
+        copy = pltpu.make_async_copy(src, dst, sems.at[len(copies)])
+        copy.start()
+        copies.append(copy)
+        return copy
+
+    def piece(rows, pieces):
+        return [pl.ds(k * rows // pieces, rows // pieces) for k in range(pieces)]
+
+    load_hidden = start(hidden, hidden_in)
+    load_cotangent = start(cotangent, cotangent_in)
+    load_tokens = start(tokens, tokens_in)
+    load_gate = start(grad_gate, gate_in)
+    load_up = start(grad_up, up_in)
+    smalls = [start(src, small_in.at[k]) for k, src in enumerate((primal, tangent, input_cotangent))]
+    waits = []
+
+    def product(left_side, right_side, rows, out, pieces):
+        for part in piece(left_side.shape[0], pieces):
+            rows[part] = (dot(left_side[part], right_side[...]) * normalizer).astype(BF16)
+            waits.append(start(rows.at[part], out.at[part]))
+
+    load_hidden.wait()
+    load_cotangent.wait()
+    product(hidden_in, cotangent_in, down_rows, down_out, 2)
+    load_tokens.wait()
+    load_gate.wait()
+    product(tokens_in, gate_in, gate_rows, gate_out, 2)
+    for k, dst in enumerate((primal_out, tangent_out, input_out)):
+        smalls[k].wait()
+        waits.append(start(small_in.at[k], dst))
+    load_up.wait()
+    product(tokens_in, up_in, up_rows, up_out, 4)
+    for copy in waits:
+        copy.wait()
 
 
 def on_device(*arguments):
@@ -512,8 +699,9 @@
     outs = pl.pallas_call(
         main_kernel,
         out_shape=[shape((small, features), BF16)] * 3
-        + [shape((2, half_rows, units), BF16)] * 3
-        + [shape((2, half_rows, features), BF16)] * 2,
+        + [shape((units, 2 * half_rows), BF16)]
+        + [shape((2, half_rows, units), BF16)] * 2
+        + [shape((features, 2 * half_rows), BF16), shape((2, half_rows, features), BF16)],
         in_specs=[hbm] * 9,
         out_specs=[hbm] * 8,
         scratch_shapes=[
@@ -532,22 +720,36 @@
             vm((5, 2, block, units), BF16),
             vm((5, 2, block, units), BF16),
             vm((2, 2, block, units), F32),
+            vm((2, 2, block, units), F32),
+            vm((2, 2, block, units), F32),
             vm((4, 2, half_rows, units), BF16),
             vm((4, 2, half_rows, half_features), F32),
             vm((4, 2, half_rows, half_features), F32),
             vm((4, 2, half_rows, half_features), F32),
-            vm((4, 2, half_rows, half_features), BF16),
-            vm((4, 2, block, half_features), BF16),
-            vm((4, 2, block, half_features), BF16),
-            vm((4, 2, block, half_features), BF16),
-            vm((4, 2, block, half_features), BF16),
-            vm((2, 2, block, half_features), F32),
-            vm((2, 2, block, half_features), F32),
-            vm((2, 2, block, half_features), F32),
-            vm((2, 2, small, half_features), F32),
+            vm((2, block, half_features), F32),
+            vm((2, block, half_features), F32),
+            vm((2, block, half_features), F32),
+            vm((2, block, half_features), F32),
+            vm((2, half_rows, half_features), BF16),
+            vm((2, block, half_features), BF16),
+            vm((2, block, half_features), BF16),
+            vm((2, block, half_features), BF16),
+            vm((2, block, half_features), BF16),
+            vm((2, 2, half_rows, half_features // 2), BF16),
+            vm((2, 2, block, half_features // 2), BF16),
+            vm((2, 2, block, half_features // 2), BF16),
+            vm((2, 2, block, half_features // 2), BF16),
+            vm((2, 2, block, half_features // 2), BF16),
+            vm((3, 2, block, half_features), F32),
+            vm((3, 2, block, half_features), F32),
+            vm((3, 2, block, half_features), F32),
+            vm((3, 2, small, half_features), F32),
             vm((3, small, features), BF16),
-            pltpu.SemaphoreType.DMA((120,)),
-            pltpu.SemaphoreType.DMA((120,)),
+            vm((features, 2 * half_rows), BF16),
+            vm((units, 2 * half_rows), BF16),
+            vm((2, half_rows, features), F32),
+            pltpu.SemaphoreType.DMA((144,)),
+            pltpu.SemaphoreType.DMA((144,)),
             pltpu.SemaphoreType.DMA((32,)),
         ],
         compiler_params=pltpu.CompilerParams(
@@ -561,14 +763,27 @@
         name="linearized_block",
     )(*arguments)
     primal, tangent, input_cotangent, hidden, grad_gate, grad_up, rows_in, cot = outs
-    flat = lambda value: value.reshape(2 * half_rows, value.shape[2])
-    vmem = pl.BlockSpec(memory_space=pltpu.VMEM)
-    normalizer = 1.0 / math.sqrt(2 * half_rows)
-    gate_gradient, up_gradient, down_gradient = pl.pallas_call(
-        functools.partial(gradient_kernel, normalizer),
-        out_shape=[shape((features, units), BF16)] * 2 + [shape((units, features), BF16)],
-        in_specs=[vmem] * 5,
-        out_specs=[vmem] * 3,
+    total_rows = 2 * half_rows
+    flat = lambda value: value.reshape(total_rows, value.shape[2])
+    return pl.pallas_call(
+        functools.partial(gradient_kernel, 1.0 / math.sqrt(total_rows)),
+        out_shape=[shape((small, features), BF16)] * 3
+        + [shape((features, units), BF16)] * 2
+        + [shape((units, features), BF16)],
+        in_specs=[hbm] * 8,
+        out_specs=[hbm] * 6,
+        scratch_shapes=[
+            vm((features, total_rows), BF16),
+            vm((units, total_rows), BF16),
+            vm((total_rows, features), BF16),
+            vm((total_rows, units), BF16),
+            vm((total_rows, units), BF16),
+            vm((3, small, features), BF16),
+            vm((features, units), BF16),
+            vm((features, units), BF16),
+            vm((units, features), BF16),
+            pltpu.SemaphoreType.DMA((24,)),
+        ],
         compiler_params=pltpu.CompilerParams(vmem_limit_bytes=60 << 20),
         cost_estimate=pl.CostEstimate(
             flops=6 * 2 * half_rows * features * units,
@@ -576,8 +791,16 @@
             transcendentals=0,
         ),
         name="gradients",
-    )(flat(rows_in), flat(cot), flat(hidden), flat(grad_gate), flat(grad_up))
-    return (primal, tangent, input_cotangent, gate_gradient, up_gradient, down_gradient)
+    )(
+        rows_in,
+        hidden,
+        flat(cot),
+        flat(grad_gate),
+        flat(grad_up),
+        primal,
+        tangent,
+        input_cotangent,
+    )
 
 
 def solution(mesh):

time: 95.1 us -> 88.1 us (0.926)
  Pallas kernels: 92.5 us -> 87.1 us
  local copies, waits for them, and re-layouts: 1.87 us -> 0 us
    pallas_call x1, Pallas kernels: 85.8 us -> 81.3 us  [on_device(): pl.pallas_call(main_kernel, out_shape=[shape((small, features), BF16)] *...]
    unnamed x9 -> x0, local copies, waits for them, and re-layouts: 1.87 us -> none
where the time goes in v2:
time: 88.1 us; the launch traced here: 87.9 us
  Pallas kernels  87.1 us (99%)
    pallas_call x1, Pallas kernels, on_device(): pl.pallas_call(main_kernel, out_shape=[shape((small, features), BF16)] *...  81.3 us
    pallas_call x1, Pallas kernels, on_device(): pl.pallas_call(functools.partial(gradient_kernel, 1.0 / math.sqrt(total_r...  5.83 us

profile of v2, /device:TPU:1, one launch (start us, length us, event | category | flops | bytes accessed | tf_op | source)
XLA Modules:
  0.0 87.9 jit_solution(14261072987895501652)
XLA Ops:
  0.6 81.3 %linearized_block.1 = (bf16[24,1024]{1,0:T(8,128)(2,1)}, bf16[24,1024]{1,0:T(8,128)(2,1)}, bf16[24,1024]{1,0:T(8,128)(2,1)}, bf16[896,384]{1,0:T(8,128)(2,1)}, b...) custom-call(bf16[192,1024]{1,0:T(8,128)(2,1)} %tokens.1, ...), custom_call_target="tpu_custom_call" | custom-call | flops 8455716864 | bytes 11010048 | tf_op jit(solution)/shard_map/linearized_block/pallas_call | solution.py:699
  81.9 5.8 %gradients.1 = (bf16[24,1024]{1,0:T(8,128)(2,1)}, bf16[24,1024]{1,0:T(8,128)(2,1)}, bf16[24,1024]{1,0:T(8,128)(2,1)}, bf16[1024,896]{1,0:T(8,128)(2,1)}, bf16[10...) custom-call(bf16[1024,384]{1,0:T(8,128)(2,1)} %get-tuple-element.14.tokens, bf16[896,384]{1,0:T(8,128)(2,1)} %get-tuple-element.15.hidden, ...), custom_call_target="tpu_custom_call" | custom-call | flops 2113929216 | bytes 8650752 | tf_op jit(solution)/shard_map/gradients/pallas_call | solution.py:768

commit v3 on v2

--- a/solution.py
+++ b/solution.py
@@ -500,25 +500,27 @@
         outs = (primal_out, input_out, tangent_out)
         stores.append(cp.local(result.at[unit], outs[unit]))
 
+    def drain(keep):
+        while len(cp.sent) > keep:
+            cp.sent.pop(0).wait_send()
+
     load_wide[0].wait()
     load_wide[1].wait()
     forward_sums(0, 0)
     ring[0].start()
-
     pair_copy.wait_recv()
     cot[0, y_rows(0)] = cot_pair[...].astype(BF16)
     cot_cross = cot_over_dp()
     cot_next = [cot_send(0, 0, y_next)]
-    cot_prev = [cot_send(0, 0, y_prev)]
-
     load_tangent.wait()
     load_wide[2].wait()
     load_wide[3].wait()
     forward_tangents(1, 0)
-    ring[1].start()
+    cot_prev = [cot_send(0, 0, y_prev)]
     rows_b = send_rows(1)
     ring[0].merge()
     rows_a.wait_recv()
+    ring[1].start()
     rows_c = forward_rows(0)
     cot_next[0].wait_recv()
     cot_far = [cot_send(0, 3, y_next)]
@@ -529,17 +531,16 @@
     rows_c.wait_recv()
     forward_sums(2, 1)
     ring[2].start()
-    ring[1].merge()
     cot_far[0].wait_recv()
     cot_siblings = [cot_send(0, shift, sibling) for shift in (1, 2, 3)]
+    finish_x(0)
     cot_next[1].wait_recv()
     cot_far.append(cot_send(1, 3, y_next))
-    finish_x(0)
     for copy in cot_siblings:
         copy.wait_recv()
     load_down[0].wait()
+    rows_b.wait_recv()
     store_partial(4, 0, dot_trans(cot[0], down[0]))
-    rows_b.wait_recv()
     rows_d = forward_rows(1)
     cot_prev[1].wait_recv()
     cot_far[1].wait_recv()
@@ -553,66 +554,72 @@
     ring[3].start()
     finish_x(2)
     ring[4].merge()
+    ring[1].merge()
     z_copies[0].wait_recv()
     hidden_block(0)
-    tokens_turned[...] = rows_in[:, 0].reshape(2 * half_rows, features).T
-    stores.append(cp.local(tokens_turned, tokens_out))
-    for half in range(2):
-        stores.append(cp.local(cot.at[half], cotangent_out.at[half]))
     ring[3].merge()
     finish_x(4)
-    finish_x(3)
-    finish_x(1)
+    tokens_turned[...] = rows_in[:, 0].reshape(2 * half_rows, features).T
+    drain(24)
     z_copies[2].wait_recv()
     hidden_block(1)
     hidden_gather.start()
+    finish_x(3)
     hidden_gather.forward()
     z_copies[4].wait_recv()
     grad_block(1)
     grad_block(0)
+    finish_x(1)
+    hidden_gather.wait()
+    load_down[1].wait()
+    hidden_turned[...] = whole[0].reshape(2 * half_rows, whole.shape[3]).T
+    drain(16)
     z_copies[3].wait_recv()
+    out_compute(0)
+    base_compute(0)
+    grad_gather[1].forward()
     tangent_block(1)
-    hidden_gather.wait()
-    grad_gather[1].forward()
-    load_down[1].wait()
-    out_compute(0)
-    z_copies[1].wait_recv()
-    tangent_block(0)
-    grad_gather[1].forward_far()
     out_start(0)
     grad_gather[0].forward()
-    base_compute(0)
+    for half in range(2):
+        stores.append(cp.local(cot.at[half], cotangent_out.at[half]))
+    grad_gather[1].forward_far()
+    base_compute(1)
+    z_copies[1].wait_recv()
     tangent_gather[1].forward()
-    base_compute(1)
+    tangent_block(0)
+    grad_gather[0].wait()
+    drain(24)
     out_merge(0)
-    tangent_gather[0].forward()
     grad_gather[1].wait()
-    grad_gather[0].wait()
-    out_compute(1)
-    out_dp(0)
     tangent_gather[1].wait()
     out_compute(3)
+    out_compute(1)
+    out_start(3)
+    tangent_gather[0].forward()
+    out_dp(0)
     out_start(1)
-    out_start(3)
+    out_merge(3)
     tangent_gather[0].wait()
     out_compute(2)
     out_merge(1)
+    drain(16)
+    out_dp(3)
     out_start(2)
-    out_merge(3)
-    hidden_turned[...] = whole[0].reshape(2 * half_rows, whole.shape[3]).T
-    stores.append(cp.local(hidden_turned, hidden_out))
-    out_dp(1)
-    out_merge(2)
-    out_dp(3)
-    out_swap(0)
     for half in range(2):
         stores.append(cp.local(whole.at[2 + half, 0], grad_gate_out.at[half]))
         stores.append(cp.local(whole.at[2 + half, 1], grad_up_out.at[half]))
+    out_swap(0)
+    out_dp(1)
+    stores.append(cp.local(tokens_turned, tokens_out))
+    drain(12)
+    out_merge(2)
+    out_swap(2)
+    out_swap(1)
     out_store(0)
-    out_swap(1)
-    out_swap(2)
+    out_store(2)
+    stores.append(cp.local(hidden_turned, hidden_out))
     out_store(1)
-    out_store(2)
 
     for copy in cp.sent:
         copy.wait_send()

time: 88.1 us -> 85.7 us (0.973)
  Pallas kernels: 87.1 us -> 84.8 us
    pallas_call x1, Pallas kernels: 81.3 us -> 79 us  [on_device(): pl.pallas_call(main_kernel, out_shape=[shape((small, features), BF16)] *...]
where the time goes in v3:
time: 85.7 us; the launch traced here: 85.6 us
  Pallas kernels  84.8 us (99%)
    pallas_call x1, Pallas kernels, on_device(): pl.pallas_call(main_kernel, out_shape=[shape((small, features), BF16)] *...  79 us
    pallas_call x1, Pallas kernels, on_device(): pl.pallas_call(functools.partial(gradient_kernel, 1.0 / math.sqrt(total_r...  5.83 us

profile of v3, /device:TPU:1, one launch (start us, length us, event | category | flops | bytes accessed | tf_op | source)
XLA Modules:
  0.0 85.6 jit_solution(16330953431538895368)
XLA Ops:
  0.6 79.0 %linearized_block.1 = (bf16[24,1024]{1,0:T(8,128)(2,1)}, bf16[24,1024]{1,0:T(8,128)(2,1)}, bf16[24,1024]{1,0:T(8,128)(2,1)}, bf16[896,384]{1,0:T(8,128)(2,1)}, b...) custom-call(bf16[192,1024]{1,0:T(8,128)(2,1)} %tokens.1, ...), custom_call_target="tpu_custom_call" | custom-call | flops 8455716864 | bytes 11010048 | tf_op jit(solution)/shard_map/linearized_block/pallas_call | solution.py:706
  79.6 5.8 %gradients.1 = (bf16[24,1024]{1,0:T(8,128)(2,1)}, bf16[24,1024]{1,0:T(8,128)(2,1)}, bf16[24,1024]{1,0:T(8,128)(2,1)}, bf16[1024,896]{1,0:T(8,128)(2,1)}, bf16[10...) custom-call(bf16[1024,384]{1,0:T(8,128)(2,1)} %get-tuple-element.14.tokens, bf16[896,384]{1,0:T(8,128)(2,1)} %get-tuple-element.15.hidden, ...), custom_call_target="tpu_custom_call" | custom-call | flops 2113929216 | bytes 8650752 | tf_op jit(solution)/shard_map/gradients/pallas_call | solution.py:775

commit v4 on v2

--- a/solution.py
+++ b/solution.py
@@ -201,11 +201,10 @@
     primal_out,
     tangent_out,
     input_out,
-    hidden_out,
+    down_gradient,
     grad_gate_out,
     grad_up_out,
     tokens_out,
-    cotangent_out,
     wide,
     down,
     rows_in,
@@ -247,7 +246,7 @@
     swap_recv,
     result,
     tokens_turned,
-    hidden_turned,
+    down_rows,
     tangent_base,
     send_sems,
     recv_sems,
@@ -296,6 +295,7 @@
     rows_a = send_rows(0)
 
     small = block // 2
+    normalizer = 1.0 / math.sqrt(2 * half_rows)
     load_cot.wait()
     my_small = pl.ds(pl.multiple_of(c * small, 8), small)
     cot_pair[my_small] = cot_own[...].astype(F32)
@@ -500,24 +500,23 @@
         outs = (primal_out, input_out, tangent_out)
         stores.append(cp.local(result.at[unit], outs[unit]))
 
+    load_down[0].wait()
     load_wide[0].wait()
     load_wide[1].wait()
     forward_sums(0, 0)
     ring[0].start()
-
     pair_copy.wait_recv()
     cot[0, y_rows(0)] = cot_pair[...].astype(BF16)
     cot_cross = cot_over_dp()
     cot_next = [cot_send(0, 0, y_next)]
-    cot_prev = [cot_send(0, 0, y_prev)]
-
     load_tangent.wait()
     load_wide[2].wait()
     load_wide[3].wait()
+    cot_prev = [cot_send(0, 0, y_prev)]
     forward_tangents(1, 0)
-    ring[1].start()
     rows_b = send_rows(1)
     ring[0].merge()
+    ring[1].start()
     rows_a.wait_recv()
     rows_c = forward_rows(0)
     cot_next[0].wait_recv()
@@ -529,85 +528,85 @@
     rows_c.wait_recv()
     forward_sums(2, 1)
     ring[2].start()
-    ring[1].merge()
     cot_far[0].wait_recv()
     cot_siblings = [cot_send(0, shift, sibling) for shift in (1, 2, 3)]
+    finish_x(0)
     cot_next[1].wait_recv()
     cot_far.append(cot_send(1, 3, y_next))
-    finish_x(0)
     for copy in cot_siblings:
         copy.wait_recv()
-    load_down[0].wait()
-    store_partial(4, 0, dot_trans(cot[0], down[0]))
+    ring[2].merge()
     rows_b.wait_recv()
     rows_d = forward_rows(1)
     cot_prev[1].wait_recv()
     cot_far[1].wait_recv()
+    store_partial(4, 0, dot_trans(cot[0], down[0]))
     cot_last = cp.start(cot.at[1, :, own_cols], cot.at[1, :, own_cols], sibling)
-    ring[2].merge()
+    ring[1].merge()
     cot_last.wait_recv()
+    tokens_turned[...] = rows_in[:, 0].reshape(2 * half_rows, features).T
+    rows_d.wait_recv()
     store_partial(4, 1, dot_trans(cot[1], down[0]))
     ring[4].start()
-    rows_d.wait_recv()
-    forward_tangents(3, 1)
-    ring[3].start()
     finish_x(2)
     ring[4].merge()
     z_copies[0].wait_recv()
+    forward_tangents(3, 1)
+    ring[3].start()
+    finish_x(4)
     hidden_block(0)
-    tokens_turned[...] = rows_in[:, 0].reshape(2 * half_rows, features).T
-    stores.append(cp.local(tokens_turned, tokens_out))
-    for half in range(2):
-        stores.append(cp.local(cot.at[half], cotangent_out.at[half]))
     ring[3].merge()
-    finish_x(4)
-    finish_x(3)
     finish_x(1)
     z_copies[2].wait_recv()
     hidden_block(1)
     hidden_gather.start()
-    hidden_gather.forward()
     z_copies[4].wait_recv()
     grad_block(1)
+    hidden_gather.forward()
+    finish_x(3)
+    grad_gather[1].forward()
+    z_copies[1].wait_recv()
     grad_block(0)
+    hidden_gather.wait()
+    out_compute(0)
+    hidden_turned = whole[0].reshape(2 * half_rows, whole.shape[3]).T
+    down_rows[...] = (
+        dot(hidden_turned, cot[...].reshape(2 * half_rows, features)) * normalizer
+    ).astype(BF16)
+    stores.append(cp.local(down_rows, down_gradient))
+    grad_gather[1].forward_far()
+    grad_gather[0].forward()
+    out_start(0)
+    load_down[1].wait()
     z_copies[3].wait_recv()
     tangent_block(1)
-    hidden_gather.wait()
-    grad_gather[1].forward()
-    load_down[1].wait()
-    out_compute(0)
-    z_copies[1].wait_recv()
+    grad_gather[0].wait()
     tangent_block(0)
-    grad_gather[1].forward_far()
-    out_start(0)
-    grad_gather[0].forward()
+    tangent_gather[1].forward()
+    out_merge(0)
+    grad_gather[1].wait()
+    out_compute(1)
+    base_compute(1)
+    tangent_gather[1].wait()
+    tangent_gather[0].forward()
+    out_start(1)
+    stores.append(cp.local(tokens_turned, tokens_out))
+    out_compute(3)
+    out_dp(0)
     base_compute(0)
-    tangent_gather[1].forward()
-    base_compute(1)
-    out_merge(0)
-    tangent_gather[0].forward()
-    grad_gather[1].wait()
-    grad_gather[0].wait()
-    out_compute(1)
-    out_dp(0)
-    tangent_gather[1].wait()
-    out_compute(3)
-    out_start(1)
     out_start(3)
     tangent_gather[0].wait()
+    out_merge(1)
     out_compute(2)
-    out_merge(1)
+    out_merge(3)
+    out_swap(0)
+    out_dp(1)
     out_start(2)
-    out_merge(3)
-    hidden_turned[...] = whole[0].reshape(2 * half_rows, whole.shape[3]).T
-    stores.append(cp.local(hidden_turned, hidden_out))
-    out_dp(1)
-    out_merge(2)
     out_dp(3)
-    out_swap(0)
     for half in range(2):
         stores.append(cp.local(whole.at[2 + half, 0], grad_gate_out.at[half]))
         stores.append(cp.local(whole.at[2 + half, 1], grad_up_out.at[half]))
+    out_merge(2)
     out_store(0)
     out_swap(1)
     out_swap(2)
@@ -623,8 +622,7 @@
 def gradient_kernel(
     normalizer,
     tokens,
-    hidden,
-    cotangent,
+    down_gradient,
     grad_gate,
     grad_up,
     primal,
@@ -637,14 +635,12 @@
     up_out,
     down_out,
     tokens_in,
-    hidden_in,
-    cotangent_in,
     gate_in,
     up_in,
     small_in,
     gate_rows,
     up_rows,
-    down_rows,
+    down_in,
     sems,
 ):
     copies = []
@@ -658,11 +654,10 @@
     def piece(rows, pieces):
         return [pl.ds(k * rows // pieces, rows // pieces) for k in range(pieces)]
 
-    load_hidden = start(hidden, hidden_in)
-    load_cotangent = start(cotangent, cotangent_in)
+    load_gate = start(grad_gate, gate_in)
     load_tokens = start(tokens, tokens_in)
-    load_gate = start(grad_gate, gate_in)
     load_up = start(grad_up, up_in)
+    load_down = start(down_gradient, down_in)
     smalls = [start(src, small_in.at[k]) for k, src in enumerate((primal, tangent, input_cotangent))]
     waits = []
 
@@ -671,12 +666,11 @@
             rows[part] = (dot(left_side[part], right_side[...]) * normalizer).astype(BF16)
             waits.append(start(rows.at[part], out.at[part]))
 
-    load_hidden.wait()
-    load_cotangent.wait()
-    product(hidden_in, cotangent_in, down_rows, down_out, 2)
     load_tokens.wait()
     load_gate.wait()
-    product(tokens_in, gate_in, gate_rows, gate_out, 2)
+    product(tokens_in, gate_in, gate_rows, gate_out, 4)
+    load_down.wait()
+    waits.append(start(down_in, down_out))
     for k, dst in enumerate((primal_out, tangent_out, input_out)):
         smalls[k].wait()
         waits.append(start(small_in.at[k], dst))
@@ -699,11 +693,11 @@
     outs = pl.pallas_call(
         main_kernel,
         out_shape=[shape((small, features), BF16)] * 3
-        + [shape((units, 2 * half_rows), BF16)]
+        + [shape((units, features), BF16)]
         + [shape((2, half_rows, units), BF16)] * 2
-        + [shape((features, 2 * half_rows), BF16), shape((2, half_rows, features), BF16)],
+        + [shape((features, 2 * half_rows), BF16)],
         in_specs=[hbm] * 9,
-        out_specs=[hbm] * 8,
+        out_specs=[hbm] * 7,
         scratch_shapes=[
             vm((4, features, units), BF16),
             vm((2, units, features), BF16),
@@ -746,7 +740,7 @@
             vm((3, 2, small, half_features), F32),
             vm((3, small, features), BF16),
             vm((features, 2 * half_rows), BF16),
-            vm((units, 2 * half_rows), BF16),
+            vm((units, features), BF16),
             vm((2, half_rows, features), F32),
             pltpu.SemaphoreType.DMA((144,)),
             pltpu.SemaphoreType.DMA((144,)),
@@ -762,7 +756,7 @@
         ),
         name="linearized_block",
     )(*arguments)
-    primal, tangent, input_cotangent, hidden, grad_gate, grad_up, rows_in, cot = outs
+    primal, tangent, input_cotangent, down_gradient, grad_gate, grad_up, rows_in = outs
     total_rows = 2 * half_rows
     flat = lambda value: value.reshape(total_rows, value.shape[2])
     return pl.pallas_call(
@@ -770,12 +764,10 @@
         out_shape=[shape((small, features), BF16)] * 3
         + [shape((features, units), BF16)] * 2
         + [shape((units, features), BF16)],
-        in_specs=[hbm] * 8,
+        in_specs=[hbm] * 7,
         out_specs=[hbm] * 6,
         scratch_shapes=[
             vm((features, total_rows), BF16),
-            vm((units, total_rows), BF16),
-            vm((total_rows, features), BF16),
             vm((total_rows, units), BF16),
             vm((total_rows, units), BF16),
             vm((3, small, features), BF16),
@@ -793,8 +785,7 @@
         name="gradients",
     )(
         rows_in,
-        hidden,
-        flat(cot),
+        down_gradient,
         flat(grad_gate),
         flat(grad_up),
         primal,

time: 88.1 us -> 85.1 us (0.966)
  Pallas kernels: 87.1 us -> 84.2 us
    pallas_call x1, Pallas kernels: 81.3 us -> 79.5 us  [on_device(): pl.pallas_call(main_kernel, out_shape=[shape((small, features), BF16)] *...]
    pallas_call x1, Pallas kernels: 5.83 us -> 4.74 us  [on_device(): pl.pallas_call(functools.partial(gradient_kernel, 1.0 / math.sqrt(total_r...]
where the time goes in v4:
time: 85.1 us; the launch traced here: 85 us
  Pallas kernels  84.2 us (99%)
    pallas_call x1, Pallas kernels, on_device(): pl.pallas_call(main_kernel, out_shape=[shape((small, features), BF16)] *...  79.5 us
    pallas_call x1, Pallas kernels, on_device(): pl.pallas_call(functools.partial(gradient_kernel, 1.0 / math.sqrt(total_r...  4.74 us

profile of v4, /device:TPU:1, one launch (start us, length us, event | category | flops | bytes accessed | tf_op | source)
XLA Modules:
  0.0 85.0 jit_solution(621184164029060179)
XLA Ops:
  0.6 79.5 %linearized_block.1 = (bf16[24,1024]{1,0:T(8,128)(2,1)}, bf16[24,1024]{1,0:T(8,128)(2,1)}, bf16[24,1024]{1,0:T(8,128)(2,1)}, bf16[896,1024]{1,0:T(8,128)(2,1)}, ...) custom-call(bf16[192,1024]{1,0:T(8,128)(2,1)} %tokens.1, ...), custom_call_target="tpu_custom_call" | custom-call | flops 8455716864 | bytes 11010048 | tf_op jit(solution)/shard_map/linearized_block/pallas_call | solution.py:693
  80.1 4.7 %gradients.1 = (bf16[24,1024]{1,0:T(8,128)(2,1)}, bf16[24,1024]{1,0:T(8,128)(2,1)}, bf16[24,1024]{1,0:T(8,128)(2,1)}, bf16[1024,896]{1,0:T(8,128)(2,1)}, bf16[10...) custom-call(bf16[1024,384]{1,0:T(8,128)(2,1)} %get-tuple-element.13.tokens, ...), custom_call_target="tpu_custom_call" | custom-call | flops 2113929216 | bytes 8650752 | tf_op jit(solution)/shard_map/gradients/pallas_call | solution.py:762
